TPU v7x, 512 devices: a whole 4x4x16 slice. The times are simulated.
512 devices in a mesh: expert: 32 (over x_hi, z), ffn: 16 (over y, x_lo, core).
Axes of the slice: x: 4 (x_hi: 2, x_lo: 2; x = x_hi * 2 + x_lo), y: 4, z: 16, core: 2. Of those that a mesh axis runs over, the one named last changes fastest.
Arguments:
- tokens: bfloat16 [4096, 7168], P('expert', 'ffn'), may hold values from -6 to 6
- routes: int32 [4096, 2], P('expert'), may hold values from 0 to 31, all different within a row; in each aligned block of 128 rows (0 to 127, 128 to 255, ...) at most 16 rows name the same one
- gate_w: bfloat16 [32, 7168, 2048], P('expert', None, 'ffn'), may hold values from -0.0625 to 0.0625
- up_w: bfloat16 [32, 7168, 2048], P('expert', None, 'ffn'), may hold values from -0.0625 to 0.0625
- down_w: bfloat16 [32, 128, 2048], P('expert', None, 'ffn'), may hold values from -2.55 to 2.25
- codes: int32 [32, 128, 128], P('expert'), may hold values from 0 to 15
- scales: float32 [32, 128], P('expert'), may hold values from 0.1 to 0.3
- hinv_panel: float32 [32, 128, 2048], P('expert', None, 'ffn'), may hold values from -0.3 to 1.5, as said below
Outputs:
- hessian: float32 [32, 2048, 2048], P('expert', 'ffn')
- panel_errors: float32 [32, 128, 128], P('expert')
- down_out: bfloat16 [32, 128, 2048], P('expert', None, 'ffn')
Inputs may be any that keep to these rules, and one draw needn't show every extreme that they name: `routes`: in each aligned block of 128 rows no expert is named by more than 16 rows, a bound that some block reaches; the 2 entries of a row differ; every expert is named by some row. `hinv_panel`: row i is zero in columns below i; its entry in column i lies between 0.5 and 1.5, the others between -0.3 and 0.3.
All inputs are finite; a program needn't handle non-finite values.
Results may differ from a plain program's by a relative error of at most 0.0047.
Values may be sent and summed in bfloat16 or wider, within the bound.
A program may use at most 64 MiB of HBM per device.

v0:
```python
import jax
import jax.numpy as jnp
from jax import lax
from jax.sharding import PartitionSpec as P


def spread(shard, axis, root):
    mine = lax.axis_index(axis) == root
    return lax.psum(jnp.where(mine, shard, jnp.zeros_like(shard)), axis)


def panel_solve(w, q, u):
    target = w - q
    rows_count = target.shape[0]
    width = target.shape[1]
    zero = jnp.zeros((), jnp.int32)

    def column_step(index, err):
        col = jnp.asarray(index).astype(jnp.int32)
        factor_col = lax.dynamic_slice(u, (zero, col), (width, 1))
        pivot = lax.dynamic_slice(u, (col, col), (1, 1))
        rhs = lax.dynamic_slice(target, (zero, col), (rows_count, 1))
        partial_sum = jnp.dot(
            err, factor_col, precision=lax.Precision.HIGHEST, preferred_element_type=jnp.float32
        )
        fresh = (rhs - partial_sum) / pivot
        return lax.dynamic_update_slice(err, fresh, (zero, col))

    start = jnp.zeros((rows_count, width), target.dtype)
    return lax.fori_loop(0, width, column_step, start)


def slot_sources(routes, experts, capacity):
    flat = routes.reshape(-1)
    count = flat.shape[0]
    top_k = routes.shape[1]
    ids = jnp.arange(experts)
    onehot = (flat[:, None] == ids[None, :]).astype(jnp.float32)
    positions = jnp.arange(count)
    earlier = (positions[:, None] > positions[None, :]).astype(jnp.float32)
    before = jnp.dot(
        earlier, onehot, precision=lax.Precision.HIGHEST, preferred_element_type=jnp.float32
    )
    ranks = jnp.sum(before * onehot, axis=1).astype(jnp.int32)
    target = flat * capacity + ranks
    every = jnp.arange(experts * capacity)
    match = target[None, :] == every[:, None]
    local_tok = jnp.arange(count) // top_k
    source = jnp.sum(jnp.where(match, local_tok[None, :], 0), axis=1)
    valid = jnp.any(match, axis=1)
    return (source, valid)


def pack_rows(data, source, valid, experts, capacity):
    picked = jnp.take(data, source, axis=0)
    picked = jnp.where(valid[:, None], picked, jnp.zeros_like(picked))
    return picked.reshape(experts, capacity, data.shape[1])


def body(tokens, routes, gate_w, up_w, down_w, codes, scales, hinv_panel):
    experts = lax.axis_size("expert")
    capacity = max(2, tokens.shape[0] * routes.shape[1] * 2 // experts)
    source, valid = slot_sources(routes, experts, capacity)
    flags = valid.astype(jnp.bfloat16).reshape(experts, capacity)
    gate_m = gate_w[0]
    up_m = up_w[0]
    widened = lax.all_gather(tokens, "ffn", axis=1, tiled=True)
    packed = pack_rows(widened, source, valid, experts, capacity)
    arrived, marks = (
        lax.all_to_all(packed, "expert", split_axis=0, concat_axis=0, tiled=True),
        lax.all_to_all(flags, "expert", split_axis=0, concat_axis=0, tiled=True),
    )
    rows = arrived.reshape(experts * capacity, arrived.shape[2])
    gate = jnp.dot(rows, gate_m, preferred_element_type=jnp.float32)
    up = jnp.dot(rows, up_m, preferred_element_type=jnp.float32)
    hidden = (jax.nn.silu(gate) * up).astype(jnp.bfloat16)
    total = jnp.sum(marks.astype(jnp.float32))
    hess_rows = lax.dot_general(
        hidden,
        lax.all_gather(hidden, "ffn", axis=1, tiled=True),
        (((0,), (0,)), ((), ())),
        preferred_element_type=jnp.float32,
    )
    hessian = (hess_rows * (2.0 / total))[None]
    weights = down_w[0]
    factor = hinv_panel[0]
    width = codes.shape[2]
    local_cols = weights.shape[1]
    quant = scales[0][:, None] * (codes[0] - 8).astype(jnp.float32)
    w_panel, u_block = (spread(weights.astype(jnp.float32), "ffn", 0), spread(factor, "ffn", 0))
    err = panel_solve(w_panel, quant, u_block)
    rest = weights.astype(jnp.float32) - jnp.dot(
        err, factor, precision=lax.Precision.HIGHEST, preferred_element_type=jnp.float32
    )
    padded = jnp.concatenate(
        [quant, jnp.zeros((quant.shape[0], local_cols - width), jnp.float32)], axis=1
    )
    global_col = lax.axis_index("ffn") * local_cols + jnp.arange(local_cols)
    updated = jnp.where(global_col[None, :] < width, padded, rest).astype(jnp.bfloat16)
    return (hessian, err[None], updated[None])


def solution(mesh):
    return jax.shard_map(
        body,
        mesh=mesh,
        in_specs=(
            P("expert", "ffn"),
            P("expert", None),
            P("expert", None, "ffn"),
            P("expert", None, "ffn"),
            P("expert", None, "ffn"),
            P("expert", None, None),
            P("expert", None),
            P("expert", None, "ffn"),
        ),
        out_specs=(P("expert", "ffn", None), P("expert", None, None), P("expert", None, "ffn")),
        check_vma=False,
    )
```

profile of v0, /device:TPU:1, one launch (start us, length us, event | category | flops | bytes accessed | tf_op | source)
XLA Modules:
  0.0 623.6 jit_solution(15275965786678217155)
XLA Ops:
  9.9 18.5 %all-to-all-start.1 = ((bf16[32,1,16]{2,1,0:T(2,128)(2,1)}), bf16[32,1,16]{2,1,0:T(2,128)(2,1)S(1)}, u32[]{:S(2)}, u32[]{:S(2)}) async-start(bf16[32,1,16]{2,1,0:T(2,128)(2,1)} %reshape.121), calls=%async_computation.1 | async-start | bytes 32768 | tf_op jit(solution)/shard_map/all_to_all | solution.py:71
  28.8 28.3 %all-gather.3.cloned.1.call-done = bf16[128,7168]{0,1:T(8,128)(2,1)} async-done(((bf16[128,448]{0,1:T(8,128)(2,1)}), bf16[128,7168]{0,1:T(8,128)(2,1)}) %all-gather.3.cloned.1.call-update) | async-done | bytes 1835024 | tf_op jit(solution)/shard_map/all_gather | solution.py:67
  57.1 3.9 copy.30
  61.0 15.5 %gather_fusion = bf16[512,7168]{1,0:T(8,128)(2,1)} fusion(bf16[128,7168]{1,0:T(8,128)(2,1)} %copy.30, s32[1024]{0:T(1024)S(1)} %pad_clamp_fusion), kind=kCustom, calls=%fused_computation | custom fusion | bytes 14682112 | tf_op jit(solution)/shard_map/jit(_take)/gather | solution.py:55
  76.5 7.0 %select_select_fusion = bf16[32,16,7168]{2,1,0:T(8,128)(2,1)} fusion(bf16[32,16,7168]{2,1,0:T(8,128)(2,1)} %bitcast.55, pred[32,16]{1,0:T(8,128)(4,1)S(1)} %compare_and_fusion, pred[32,16]{1,0:T(8,128)(4,1)S(1)} %broadcast_in_dim.60), kind=kLoop, calls=%fused_computation.6 | loop fusion | flops 7340032 | bytes 14681088 | tf_op jit(solution)/shard_map/jit(_where)/select_n | solution.py:56
  83.6 14.7 %all-to-all-start = ((bf16[32,16,7168]{2,1,0:T(8,128)(2,1)}), bf16[32,16,7168]{2,1,0:T(8,128)(2,1)}, u32[]{:S(2)}, u32[]{:S(2)}) async-start(bf16[32,16,7168]{2,1,0:T(8,128)(2,1)} %select_select_fusion), calls=%async_computation | async-start | bytes 14680064 | tf_op jit(solution)/shard_map/all_to_all | solution.py:70
  100.6 140.5 %all-reduce.3.cloned.1.call-done = (f32[128,128]{1,0:T(8,128)}, f32[128,128]{1,0:T(8,128)}) async-done(((f32[128,128]{1,0:T(8,128)}, f32[128,128]{1,0:T(8,128)}), (f32[128,128]{1,0:T(8,128)}, f32[128,128]{1,0:T(8,128)})) %all-reduce.3.cloned.1.call-update) | async-done | bytes 131088 | tf_op jit(solution)/shard_map/psum | solution.py:9
  241.1 0.9 fusion.21
  242.1 0.9 copy.34
  243.1 174.2 %all-to-all-done = bf16[32,16,7168]{2,1,0:T(8,128)(2,1)} async-done(((bf16[32,16,7168]{2,1,0:T(8,128)(2,1)}), bf16[32,16,7168]{2,1,0:T(8,128)(2,1)}, u32[]{:S(2)}, u32[]{:S(2)}) %all-to-all-start) | async-done | bytes 7340064 | tf_op jit(solution)/shard_map/all_to_all | solution.py:70
  417.3 5.3 fusion.7
  422.6 5.8 fusion.12
  428.4 183.9 %while.13 = (s32[]{:T(128)}, f32[128,128]{0,1:T(8,128)S(1)}, f32[128,128]{0,1:T(8,128)S(1)}, f32[128,128]{0,1:T(8,128)S(1)}, s32[]{:T(128)}, /*index=5*/s32[]{:T(128)}) while((s32[]{:T(128)}, f32[128,128]{0,1:T(8,128)S(1)}, f32[128,128]{0,1:T(8,128)S(1)}, f32[128,128]{0,1:T(8,128)S(1)}, s32[]{:T(128)}, /*index=5*/s32[]{:T(128)}) %tuple.38), condition=%wide.region_7.8_spmd, body=%wide.region_6.7_spmd.sunk | while | flops 196866 | bytes 69717 | solution.py:30
  430.5 0.8 fusion.34
  431.9 0.8 fusion.34
  433.3 0.8 fusion.34
  434.8 0.8 fusion.34
  443.4 0.8 fusion.34
  447.7 0.8 fusion.34
  450.6 0.8 fusion.34
  459.2 0.8 fusion.34
  460.6 0.8 fusion.34
  462.1 0.8 fusion.34
  463.5 0.8 fusion.34
  466.4 0.8 fusion.34
  467.8 0.8 fusion.34
  469.3 0.8 fusion.34
  470.7 0.8 fusion.34
  479.3 0.8 fusion.34
  480.8 0.8 fusion.34
  613.1 0.9 fusion.17
  614.0 3.1 fusion.4
  (406 shorter events, 173.2 us)
Async XLA Ops:
  7.2 410.1 %copy-start = (bf16[1,7168,128]{2,1,0:T(8,128)(2,1)S(1)}, bf16[1,7168,128]{2,1,0:T(8,128)(2,1)}, u32[]{:S(2)}) copy-start(bf16[1,7168,128]{2,1,0:T(8,128)(2,1)} %param.12) | copy-start | bytes 5505028
  7.2 49.9 %all-gather.3.cloned.1.call-start = ((), (), s32[]{:S(2)}) async-start(), calls=%async_computation.2 | async-start | bytes 1949696 | tf_op jit(solution)/shard_map/all_gather | solution.py:67
  9.9 73.6 %all-to-all-start.1 = ((bf16[32,1,16]{2,1,0:T(2,128)(2,1)}), bf16[32,1,16]{2,1,0:T(2,128)(2,1)S(1)}, u32[]{:S(2)}, u32[]{:S(2)}) async-start(bf16[32,1,16]{2,1,0:T(2,128)(2,1)} %reshape.121), calls=%async_computation.1 | async-start | bytes 32768 | tf_op jit(solution)/shard_map/all_to_all | solution.py:71
  83.6 14.8 %copy-start.1 = (f32[1,128,128]{2,1,0:T(8,128)S(1)}, f32[1,128,128]{2,1,0:T(8,128)}, u32[]{:S(2)}) copy-start(f32[1,128,128]{2,1,0:T(8,128)} %param.17) | copy-start | bytes 196612
  83.6 14.8 %copy-start.3 = (bf16[1,128,128]{2,1,0:T(8,128)(2,1)S(1)}, bf16[1,128,128]{2,1,0:T(8,128)(2,1)}, u32[]{:S(2)}) copy-start(bf16[1,128,128]{2,1,0:T(8,128)(2,1)} %param.14) | copy-start | bytes 98308
  83.6 157.6 %copy-start.2 = (s32[1,128,128]{2,1,0:T(8,128)S(1)}, s32[1,128,128]{2,1,0:T(8,128)}, u32[]{:S(2)}) copy-start(s32[1,128,128]{2,1,0:T(8,128)} %param.15) | copy-start | bytes 196612
  83.6 157.6 %copy-start.4 = (f32[1,128]{1,0:T(1,128)S(1)}, f32[1,128]{1,0:T(1,128)}, u32[]{:S(2)}) copy-start(f32[1,128]{1,0:T(1,128)} %param.16) | copy-start | bytes 1540
  83.6 333.7 %all-to-all-start = ((bf16[32,16,7168]{2,1,0:T(8,128)(2,1)}), bf16[32,16,7168]{2,1,0:T(8,128)(2,1)}, u32[]{:S(2)}, u32[]{:S(2)}) async-start(bf16[32,16,7168]{2,1,0:T(8,128)(2,1)} %select_select_fusion), calls=%async_computation | async-start | bytes 14680064 | tf_op jit(solution)/shard_map/all_to_all | solution.py:70
  98.3 142.8 %all-reduce.3.cloned.1.call-start = ((), (), s32[]{:S(2)}) async-start(), calls=%async_computation.4 | async-start | bytes 262144 | tf_op jit(solution)/shard_map/psum | solution.py:9
  99.1 514.9 %all-gather.5.cloned.1.call-start = ((), (), s32[]{:S(2)}) async-start(), calls=%async_computation.3 | async-start | bytes 2228224 | tf_op jit(solution)/shard_map/all_gather | solution.py:80
  417.3 5.3 copy-start.5
Sparse Core Ops, SparseCore 0:
  10.2 46.9 all-gather.2
  102.7 138.4 all-reduce.2
  428.5 43.4 all-gather.4
where the time goes:
time: 632 us; the launch traced here: 624 us
  waiting for transfers between devices  344 us (54%)
  matrix products  117 us (19%)
  local copies, waits for them, and re-layouts  102 us (16%)
  starting transfers between devices  33.5 us (5%)
  between operations  14.6 us (2%)
  other arithmetic  9.58 us (2%)
    all_to_all x1, waiting for transfers between devices, body(): lax.all_to_all(packed, 'expert', split_axis=0, concat_axis=0, tiled=True)  174 us
    psum x1, waiting for transfers between devices, spread(): return lax.psum(jnp.where(mine, shard, jnp.zeros_like(shard)), axis)  140 us
    dot_general x128, matrix products, column_step(): jnp.dot(err, factor_col, precision=lax.Precision.HIGHEST, preferred_eleme...  102 us
    dynamic_slice x128, local copies, waits for them, and re-layouts, column_step(): pivot = lax.dynamic_slice(u, (col, col), (1, 1))  75.3 us
    all_gather x1, waiting for transfers between devices, body(): widened = lax.all_gather(tokens, 'ffn', axis=1, tiled=True)  28.3 us
    all_to_all x1, starting transfers between devices, body(): lax.all_to_all(flags, 'expert', split_axis=0, concat_axis=0, tiled=True)  18.5 us
    gather x1, local copies, waits for them, and re-layouts, pack_rows(): picked = jnp.take(data, source, axis=0)  15.5 us
    all_to_all x1, starting transfers between devices, body(): lax.all_to_all(packed, 'expert', split_axis=0, concat_axis=0, tiled=True)  14.7 us
  transfers between devices with their start and end apart: 5, of which 3 were waited for; matrix products, arithmetic and copies ran while one was open for 34% of the time, Pallas kernels for 0%

commit v1 on v0

v1 whole, which is shorter than its diff:
```python
import jax
import jax.numpy as jnp
from jax import lax
from jax.experimental import pallas as pl
from jax.experimental.pallas import tpu as pltpu
from jax.sharding import PartitionSpec as P

MESH = pl.DeviceIdType.MESH
NZ = 16
NY = 4
CHIPS = 8
CAP = 16
FEAT = 448
WIDE = 896
FLAGGED = 1024
GROUPS = 4
ROWS = 64
CUT = 512
COLS = 128
HID = 256
HCUT = 128
HALF = ROWS // 2
Z_ORDER = (0, 1, 15, 2, 14, 3, 13, 4, 12, 5, 11, 6, 10, 7, 9, 8)

BESIDE_ROOT = (1, 2, 4, 12)

RING = 12
AT_TOK = 0
AT_GATE = 1
AT_UP = 2
AT_PANEL = 3
AT_A2A = 5
AT_ROWS = AT_A2A + NZ
AT_HID = AT_ROWS + RING * GROUPS
AT_SIB = AT_HID + RING * GROUPS
AT_COUNT = AT_SIB + GROUPS
AT_CAST = AT_COUNT + 1
N_RECV = AT_CAST
N_SEND = AT_CAST + 2 * 15


def exact(a, b):
    return jnp.dot(a, b, precision=lax.Precision.HIGHEST, preferred_element_type=jnp.float32)


def kernel(
    routes_at, tokens, gate_w, up_w, down_at, codes_at, scales_at, hinv_at,
    hess, err_out, down_out,
    routes, down_w, codes, scales, hinv,
    tok, packed, rows, weights, hid, u_panel, w_panel, count,
    send, recv, local,
):
    e = lax.axis_index("expert")
    f = lax.axis_index("ffn")
    xh, z = e // NZ, e % NZ
    y, xl, c = f // 4, (f // 2) % 2, f % 2
    chip = f // 2
    xo = 1 - xl
    yp, ym, yo = (y + 1) % NY, (y + 3) % NY, (y + 2) % NY
    sibling = (e, f + 1 - 2 * c)

    def chip_of(yy, xx):
        return yy * 2 + xx

    def peer(yy, xx):
        return (e, yy * 4 + xx * 2 + c)

    def far(z_to):
        return (((xh + c) % 2) * NZ + z_to, f)

    def copy(src, dst, at, device, send_at=None):
        return pltpu.make_async_remote_copy(
            src_ref=src,
            dst_ref=dst,
            send_sem=send.at[at if send_at is None else send_at],
            recv_sem=recv.at[at],
            device_id=device,
            device_id_type=MESH,
        )

    sent = []

    def go(src, dst, at, device):
        copy(src, dst, at, device).start()
        sent.append((src, at))

    def arrived(region, at):
        copy(region, region, at, sibling).wait_recv()

    half = pl.ds(pl.multiple_of(c * FEAT, FEAT), FEAT)
    other_half = pl.ds(pl.multiple_of((1 - c) * FEAT, FEAT), FEAT)
    own_tok = pltpu.make_async_copy(tokens, tok.at[half], local.at[0])
    own_gate = pltpu.make_async_copy(gate_w, weights.at[c, 0], local.at[1])
    own_up = pltpu.make_async_copy(up_w, weights.at[c, 1], local.at[2])
    small = [
        pltpu.make_async_copy(src, dst, local.at[4 + i])
        for i, (src, dst) in enumerate(
            [(routes_at, routes), (hinv_at, hinv), (down_at, down_w), (codes_at, codes), (scales_at, scales)]
        )
    ]
    small[0].start()
    own_tok.start()
    for one in small[1:]:
        one.start()
    own_gate.start()
    own_up.start()

    barrier = pltpu.get_barrier_semaphore()

    def greet(device):
        pl.semaphore_signal(barrier, inc=1, device_id=device, device_id_type=MESH)

    for dz in range(1, NZ):
        greet(far((z + dz) % NZ))

    @pl.when(c == 1)
    def _():
        greet(far(z))

    greet(peer(yp, xl))
    greet(peer(ym, xl))
    greet(peer(y, xo))
    greet(sibling)

    @pl.when(f == 0)
    def _():
        for other in range(1, 16):
            if other not in BESIDE_ROOT:
                greet((e, jnp.int32(other)))

    beside_root = (f == 1) | (f == 2) | (f == 4) | (f == 12)
    apart = (f != 0) & jnp.logical_not(beside_root)

    @pl.when(apart)
    def _():
        greet((e, jnp.int32(0)))

    small[0].wait()
    names = routes[...]
    experts = lax.broadcasted_iota(jnp.int32, (32, 128), 0)
    named = ((names[0:1, :] == experts) | (names[1:2, :] == experts)).astype(jnp.float32)
    earlier = (
        lax.broadcasted_iota(jnp.int32, (128, 128), 0) < lax.broadcasted_iota(jnp.int32, (128, 128), 1)
    ).astype(jnp.bfloat16)
    named_b = named.astype(jnp.bfloat16)
    rank = jnp.dot(named_b, earlier, preferred_element_type=jnp.float32)
    base = ((xh + c) % 2) * NZ
    slot = lax.broadcasted_iota(jnp.int32, (NZ * CAP, 32), 0)
    widen = (lax.broadcasted_iota(jnp.int32, (NZ * CAP, 32), 1) == base + slot // CAP).astype(jnp.bfloat16)
    rank_at = jnp.dot(widen, rank.astype(jnp.bfloat16), preferred_element_type=jnp.float32)
    named_at = jnp.dot(widen, named_b, preferred_element_type=jnp.float32)
    place = (lax.broadcasted_iota(jnp.int32, (NZ * CAP, 128), 0) % CAP).astype(jnp.float32)
    pick = jnp.where(rank_at == place, named_at, 0.0).astype(jnp.bfloat16)

    peers = NZ - 1 + 4

    @pl.when(f == 0)
    def _():
        pl.semaphore_wait(barrier, peers + 15 - len(BESIDE_ROOT))

    @pl.when(beside_root & (c == 0))
    def _():
        pl.semaphore_wait(barrier, peers)

    @pl.when((f == 1) | (apart & (c == 0)))
    def _():
        pl.semaphore_wait(barrier, peers + 1)

    @pl.when(apart & (c == 1))
    def _():
        pl.semaphore_wait(barrier, peers + 2)

    go(tokens, tok.at[half], AT_TOK, sibling)
    go(gate_w, weights.at[c, 0], AT_GATE, sibling)
    go(up_w, weights.at[c, 1], AT_UP, sibling)

    own_tok.wait()
    arrived(tok.at[other_half], AT_TOK)
    packed[:, :, :WIDE] = (
        lax.dot_general(pick, tok[...], (((1,), (1,)), ((), ())), preferred_element_type=jnp.float32)
        .astype(jnp.bfloat16)
        .reshape(NZ, CAP, WIDE)
    )
    packed[:, :, WIDE:] = (
        jnp.dot(pick, jnp.ones((128, 128), jnp.bfloat16), preferred_element_type=jnp.float32)
        .astype(jnp.bfloat16)
        .reshape(NZ, CAP, 128)
    )

    def landing(k):
        return rows.at[k // 4, chip, pl.ds((k % 4) * CAP, CAP), :]

    stay = pltpu.make_async_copy(packed.at[z], landing(0), local.at[3])

    @pl.when(c == 0)
    def _():
        stay.start()

    @pl.when(c == 1)
    def _():
        copy(packed.at[z], landing(0), AT_A2A, far(z)).start()

    for k in range(1, NZ):
        z_to = (z + Z_ORDER[k]) % NZ
        go(packed.at[z_to], landing(k), AT_A2A + k, far(z_to))

    small[1].wait()
    small[2].wait()

    @pl.when(f == 0)
    def _():
        for other in range(1, 16):
            to = (e, jnp.int32(other))
            copy(hinv, u_panel, AT_PANEL, to, AT_CAST + 2 * other - 2).start()
            copy(down_w, w_panel, AT_PANEL + 1, to, AT_CAST + 2 * other - 1).start()
        u_panel[...] = hinv[...]
        w_panel[...] = down_w[...]

    def ring(piece, at, width, cut):
        def part(yy, xx, first=0, count=ROWS, low=True, high=True):
            ref = piece(chip_of(yy, xx))
            start = 0 if low else cut
            stop = width if high else cut
            return ref.at[pl.ds(first, count), pl.ds(start, stop - start)]

        def send_own():
            mine = part(y, xl)
            go(mine, mine, at + 1, peer(yp, xl))
            go(mine, mine, at + 2, peer(ym, xl))
            go(mine, mine, at + 0, peer(y, xo))

        def second():
            arrived(part(y, xo), at + 0)
            low = part(y, xo, high=False)
            go(low, low, at + 5, peer(yp, xl))
            go(low, low, at + 6, peer(ym, xl))
            arrived(part(ym, xl), at + 1)
            on = part(ym, xl, 0, HALF)
            go(on, on, at + 3, peer(yp, xl))
            cross = part(ym, xl, low=False)
            go(cross, cross, at + 9, peer(y, xo))
            arrived(part(yp, xl), at + 2)
            on = part(yp, xl, HALF, HALF)
            go(on, on, at + 4, peer(ym, xl))
            cross = part(yp, xl, low=False)
            go(cross, cross, at + 10, peer(y, xo))

        def third():
            arrived(part(ym, xo, high=False), at + 5)
            on = part(ym, xo, 0, HALF, high=False)
            go(on, on, at + 7, peer(yp, xl))
            arrived(part(yp, xo, high=False), at + 6)
            on = part(yp, xo, HALF, HALF, high=False)
            go(on, on, at + 8, peer(ym, xl))
            arrived(part(yo, xl, 0, HALF), at + 3)
            arrived(part(yo, xl, HALF, HALF), at + 4)
            cross = part(yo, xl, low=False)
            go(cross, cross, at + 11, peer(y, xo))

        def last():
            arrived(part(ym, xo, low=False), at + 9)
            arrived(part(yp, xo, low=False), at + 10)
            arrived(part(yo, xo, 0, HALF, high=False), at + 7)
            arrived(part(yo, xo, HALF, HALF, high=False), at + 8)
            arrived(part(yo, xo, low=False), at + 11)

        return send_own, second, third, last

    def dispatch_arrived(g):
        for k in range(4 * g, 4 * g + 4):
            if k == 0:

                @pl.when(c == 0)
                def _():
                    stay.wait()

                @pl.when(c == 1)
                def _():
                    arrived(landing(0), AT_A2A)
            else:
                arrived(landing(k), AT_A2A + k)

    def hidden_units(g):
        if g == 0:
            own_gate.wait()
            own_up.wait()
            arrived(weights.at[1 - c, 0], AT_GATE)
            arrived(weights.at[1 - c, 1], AT_UP)
        total = jnp.zeros((ROWS, 2 * HID), jnp.float32)
        for s in range(CHIPS):
            span = pl.ds(s * WIDE, WIDE)
            factor = jnp.concatenate(
                [weights[0, 0, span, :], weights[1, 0, span, :], weights[0, 1, span, :], weights[1, 1, span, :]],
                axis=1,
            )
            total += jnp.dot(rows[g, s, :, :WIDE], factor, preferred_element_type=jnp.float32)
        gate, up = total[:, :HID], total[:, HID:]
        hid[c, g, chip] = (gate / (1.0 + jnp.exp(-gate)) * up).astype(jnp.bfloat16)

    def group(g):
        send_own, second, third, last = ring(lambda s: rows.at[g, s], AT_ROWS + RING * g, WIDE, CUT)
        h_own, h_second, h_third, h_last = ring(lambda s: hid.at[c, g, s], AT_HID + RING * g, HID, HCUT)

        def start():
            dispatch_arrived(g)
            send_own()

        def compute():
            last()
            hidden_units(g)
            h_own()

        def pass_on():
            h_last()
            go(hid.at[c, g], hid.at[c, g], AT_SIB + g, sibling)

        def finish():
            arrived(hid.at[1 - c, g], AT_SIB + g)

        return start, second, third, compute, h_second, h_third, pass_on, finish

    def panel():
        @pl.when(f != 0)
        def _():
            arrived(u_panel, AT_PANEL)
            arrived(w_panel, AT_PANEL + 1)

        u = u_panel[...]
        r = lax.broadcasted_iota(jnp.int32, (128, 128), 0)
        q = lax.broadcasted_iota(jnp.int32, (128, 128), 1)
        on_diag = r == q
        inverse = jnp.where(on_diag, 1.0 / jnp.where(on_diag, u, 1.0), 0.0)
        size = 1
        while size < 128:
            block = jnp.where((r // (2 * size) == q // (2 * size)) & (r // size != q // size), u, 0.0)
            inverse = inverse - exact(exact(inverse, block), inverse)
            size *= 2
            yield
        small[3].wait()
        small[4].wait()
        steps = jnp.sum(jnp.where(on_diag, scales[...], 0.0), axis=1, keepdims=True)
        quant = steps * (codes[...] - 8).astype(jnp.float32)
        err = exact(w_panel[...].astype(jnp.float32) - quant, inverse)
        err_out[...] = err
        yield
        rest = down_w[...].astype(jnp.float32) - exact(err, hinv[...])
        down_out[...] = jnp.where(f == 0, quant, rest).astype(jnp.bfloat16)

    stages = [group(g) for g in range(GROUPS)]
    solve = panel()
    for step in range(GROUPS + 7):
        for g in range(GROUPS):
            if 0 <= step - g < 8:
                stages[g][step - g]()
        next(solve, None)

    flags = rows[:, pl.ds(chip, 1), :, WIDE:].astype(jnp.float32).reshape(GROUPS * ROWS, 128)
    count[c] = jnp.broadcast_to(jnp.sum(flags, axis=0, keepdims=True), (8, 128))
    go(count.at[c], count.at[c], AT_COUNT, sibling)

    mine = hid[:, :, pl.ds(chip, 1), :, pl.ds(pl.multiple_of(c * COLS, COLS), COLS)].reshape(512, COLS)
    products = [
        lax.dot_general(
            mine, hid[:, :, s].reshape(512, HID), (((0,), (0,)), ((), ())), preferred_element_type=jnp.float32
        )
        for s in range(CHIPS)
    ]
    arrived(count.at[1 - c], AT_COUNT)
    scale = 2.0 / (count[0, 0:1, :] + count[1, 0:1, :])
    scale = jnp.concatenate([scale, scale], axis=1)
    for s in range(CHIPS):
        hess[:, s * HID : (s + 1) * HID] = products[s] * scale

    for src, at in sent:
        copy(src, src, at, sibling).wait_send()

    @pl.when(c == 1)
    def _():
        copy(packed.at[z], landing(0), AT_A2A, far(z)).wait_send()

    @pl.when(f == 0)
    def _():
        for other in range(1, 16):
            to = (e, jnp.int32(other))
            copy(hinv, u_panel, AT_PANEL, to, AT_CAST + 2 * other - 2).wait_send()
            copy(down_w, w_panel, AT_PANEL + 1, to, AT_CAST + 2 * other - 1).wait_send()


def body(tokens, routes, gate_w, up_w, down_w, codes, scales, hinv_panel):
    vmem = pl.BlockSpec(memory_space=pltpu.VMEM)
    hbm = pl.BlockSpec(memory_space=pltpu.HBM)
    hess, err, down = pl.pallas_call(
        kernel,
        out_shape=(
            jax.ShapeDtypeStruct((COLS, 2048), jnp.float32),
            jax.ShapeDtypeStruct((128, 128), jnp.float32),
            jax.ShapeDtypeStruct((128, 128), jnp.bfloat16),
        ),
        in_specs=[hbm] * 8,
        out_specs=(vmem, vmem, vmem),
        scratch_shapes=[
            pltpu.VMEM((2, 128), jnp.int32),
            pltpu.VMEM((128, 128), jnp.bfloat16),
            pltpu.VMEM((128, 128), jnp.int32),
            pltpu.VMEM((1, 128), jnp.float32),
            pltpu.VMEM((128, 128), jnp.float32),
            pltpu.VMEM((WIDE, 128), jnp.bfloat16),
            pltpu.VMEM((NZ, CAP, FLAGGED), jnp.bfloat16),
            pltpu.VMEM((GROUPS, CHIPS, ROWS, FLAGGED), jnp.bfloat16),
            pltpu.VMEM((2, 2, CHIPS * WIDE, COLS), jnp.bfloat16),
            pltpu.VMEM((2, GROUPS, CHIPS, ROWS, HID), jnp.bfloat16),
            pltpu.VMEM((128, 128), jnp.float32),
            pltpu.VMEM((128, 128), jnp.bfloat16),
            pltpu.VMEM((2, 8, 128), jnp.float32),
            pltpu.SemaphoreType.DMA((N_SEND,)),
            pltpu.SemaphoreType.DMA((N_RECV,)),
            pltpu.SemaphoreType.DMA((9,)),
        ],
        compiler_params=pltpu.CompilerParams(
            collective_id=0, has_side_effects=True, vmem_limit_bytes=62 * 1024 * 1024
        ),
        cost_estimate=pl.CostEstimate(flops=2_200_000_000, bytes_accessed=16_000_000, transcendentals=65536),
        name="calibrate",
    )(routes.T, tokens.T, gate_w[0], up_w[0], down_w[0], codes[0], scales, hinv_panel[0])
    return hess[None], err[None], down[None]


def solution(mesh):
    return jax.shard_map(
        body,
        mesh=mesh,
        in_specs=(
            P("expert", "ffn"),
            P("expert", None),
            P("expert", None, "ffn"),
            P("expert", None, "ffn"),
            P("expert", None, "ffn"),
            P("expert", None, None),
            P("expert", None),
            P("expert", None, "ffn"),
        ),
        out_specs=(P("expert", "ffn", None), P("expert", None, None), P("expert", None, "ffn")),
        check_vma=False,
    )
```

time: 632 us -> 88.4 us (0.14); the launches traced: 624 us -> 88.2 us
  waiting for transfers between devices: 344 us -> 0 us
  matrix products: 117 us -> 0 us
  local copies, waits for them, and re-layouts: 102 us -> 3.58 us
  Pallas kernels: 0 us -> 84 us
  starting transfers between devices: 33.5 us -> 0 us
  between operations: 14.6 us -> 0.66 us
  other arithmetic: 9.58 us -> 0 us
    all_to_all x2 -> x0, waiting for transfers between devices: 174 us -> none  [the longest x1 174 us: body(): lax.all_to_all(packed, 'expert', split_axis=0, concat_axis=0, tiled=True)]
    psum x1 -> x0, waiting for transfers between devices: 140 us -> none  [spread(): return lax.psum(jnp.where(mine, shard, jnp.zeros_like(shard)), axis)]
    dot_general x133 -> x0, matrix products: 117 us -> none  [the longest x128 102 us: column_step(): jnp.dot(err, factor_col, precision=lax.Precision.HIGHEST, preferred_eleme...]
    pallas_call x0 -> x1, Pallas kernels: none -> 84 us  [body(): pl.pallas_call(kernel, out_shape=(jax.ShapeDtypeStruct((COLS, 2048), jnp....]
    dynamic_slice x128 -> x0, local copies, waits for them, and re-layouts: 75.3 us -> none  [column_step(): pivot = lax.dynamic_slice(u, (col, col), (1, 1))]
    all_to_all x2 -> x0, starting transfers between devices: 33.2 us -> none  [the longest x1 18.5 us: body(): lax.all_to_all(flags, 'expert', split_axis=0, concat_axis=0, tiled=True)]
    all_gather x2 -> x0, waiting for transfers between devices: 28.3 us -> none  [the longest x1 28.3 us: body(): widened = lax.all_gather(tokens, 'ffn', axis=1, tiled=True)]
    gather x1 -> x0, local copies, waits for them, and re-layouts: 15.5 us -> none  [pack_rows(): picked = jnp.take(data, source, axis=0)]
  transfers between devices with their start and end apart: 5 -> 0, of which waited for: 3 -> 0; matrix products, arithmetic and copies ran while one was open for 34% -> 0% of each run, Pallas kernels for 0% -> 0%
where the time goes in v1:
time: 88.4 us; the launch traced here: 88.2 us
  Pallas kernels  84 us (95%)
  local copies, waits for them, and re-layouts  3.58 us (4%)
    pallas_call x1, Pallas kernels, body(): pl.pallas_call(kernel, out_shape=(jax.ShapeDtypeStruct((COLS, 2048), jnp....  84 us
    unnamed x7, local copies, waits for them, and re-layouts  3.58 us

profile of v1, /device:TPU:1, one launch (start us, length us, event | category | flops | bytes accessed | tf_op | source)
XLA Modules:
  0.0 88.2 jit_solution(14950442928208084837)
XLA Ops:
  0.6 84.0 %calibrate.1 = (f32[128,2048]{1,0:T(8,128)}, f32[128,128]{1,0:T(8,128)}, bf16[128,128]{1,0:T(8,128)(2,1)}) custom-call(s32[2,128]{1,0:T(2,128)} %bitcast.19, bf16[448,128]{1,0:T(8,128)(2,1)} %bitcast.15, bf16[7168,128]{1,0:T(8,128)(2,1)} %bitcast.13, bf16[7168,128]{1,0:T(8,128)(2,1)} %bitcast.14, bf16[128,128]{1,0:T(8,128)(2,1)} %bitcast.18, ...), custom_call_target="tpu_custom_call" | custom-call | flops 2200000000 | bytes 16000000 | tf_op jit(solution)/shard_map/calibrate/pallas_call | solution.py:392
  84.6 0.0 copy-start
  84.7 0.0 copy-start.1
  84.7 2.3 %copy.14 = f32[1,128,2048]{2,1,0:T(8,128)} copy(f32[1,128,2048]{2,1,0:T(8,128)} %bitcast.10) | data formatting | bytes 2097152
  87.0 0.0 copy-done
  87.0 0.6 copy.15
  87.6 0.0 copy-done.1
  87.6 0.6 copy.16
Async XLA Ops:
  84.6 2.3 %copy-start = (f32[128,128]{1,0:T(8,128)S(1)}, f32[128,128]{1,0:T(8,128)}, u32[]{:S(2)}) copy-start(f32[128,128]{1,0:T(8,128)} %get-tuple-element.7) | copy-start | bytes 196612
  84.7 3.0 %copy-start.1 = (bf16[128,128]{1,0:T(8,128)(2,1)S(1)}, bf16[128,128]{1,0:T(8,128)(2,1)}, u32[]{:S(2)}) copy-start(bf16[128,128]{1,0:T(8,128)(2,1)} %get-tuple-element.8) | copy-start | bytes 98308

commit v2 on v1

v2 whole, which is shorter than its diff:
```python
import jax
import jax.numpy as jnp
from jax import lax
from jax.experimental import pallas as pl
from jax.experimental.pallas import tpu as pltpu
from jax.sharding import PartitionSpec as P

MESH = pl.DeviceIdType.MESH
NZ = 16
NY = 4
CHIPS = 8
CAP = 16
FEAT = 448
WIDE = 896
CUT = 512
COLS = 128
HID = 256
HCUT = 128
Z_ORDER = ((0, 1, 15, 14), (2, 3, 13, 12), (4, 5, 11, 10), (6, 8, 7, 9))
GROUPS = len(Z_ORDER)
FIRST = tuple(sum(len(one) for one in Z_ORDER[:g]) for g in range(GROUPS))
ROWS = tuple(len(one) * CAP for one in Z_ORDER)
ROWS_RING = (True, True, True, True)
HID_RING = (True, True, True, False)
LATE = FIRST[-1] * CAP
FROM_ROOT = (2, 4, 6, 8, 10, 12, 14)

SOLVE = -1
RING = 12
AT_TOK = 0
AT_GATE = 1
AT_UP = 2
AT_PANEL = 3
AT_A2A = 5
AT_ROWS = AT_A2A + NZ
AT_HID = AT_ROWS + RING * GROUPS
AT_SIB = AT_HID + RING * GROUPS
AT_COUNT = AT_SIB + GROUPS
AT_TOTAL = AT_COUNT + NZ
AT_CAST = AT_TOTAL + 1
N_RECV = AT_CAST
N_SEND = AT_CAST + 2 * len(FROM_ROOT)
N_LOCAL = 11 + CHIPS


def exact(a, b):
    return jnp.dot(a, b, precision=lax.Precision.HIGHEST, preferred_element_type=jnp.float32)


def kernel(
    routes_at, tokens, gate_w, up_w, down_at, codes_at, scales_at, hinv_at,
    hess_out, err_out, down_out,
    hess, err_v, down_v, routes, down_w, codes, scales, hinv,
    tok, packed, rows, weights, hid, u_panel, w_panel, count, heard, total,
    send, recv, local,
):
    e = lax.axis_index("expert")
    f = lax.axis_index("ffn")
    xh, z = e // NZ, e % NZ
    y, xl, c = f // 4, (f // 2) % 2, f % 2
    chip = f // 2
    xo = 1 - xl
    yp, ym, yo = (y + 1) % NY, (y + 3) % NY, (y + 2) % NY
    sibling = (e, f + 1 - 2 * c)

    def chip_of(yy, xx):
        return yy * 2 + xx

    def peer(yy, xx):
        return (e, yy * 4 + xx * 2 + c)

    def far(z_to):
        return (((xh + c) % 2) * NZ + z_to, f)

    def copy(src, dst, at, device, send_at=None):
        return pltpu.make_async_remote_copy(
            src_ref=src,
            dst_ref=dst,
            send_sem=send.at[at if send_at is None else send_at],
            recv_sem=recv.at[at],
            device_id=device,
            device_id_type=MESH,
        )

    sent = []

    def go(src, dst, at, device):
        copy(src, dst, at, device).start()
        sent.append((src, at))

    def arrived(region, at):
        copy(region, region, at, sibling).wait_recv()

    half = pl.ds(pl.multiple_of(c * FEAT, FEAT), FEAT)
    other_half = pl.ds(pl.multiple_of((1 - c) * FEAT, FEAT), FEAT)
    own_tok = pltpu.make_async_copy(tokens, tok.at[half], local.at[0])
    own_gate = pltpu.make_async_copy(gate_w, weights.at[c, 0], local.at[1])
    own_up = pltpu.make_async_copy(up_w, weights.at[c, 1], local.at[2])
    small = [
        pltpu.make_async_copy(src, dst, local.at[4 + i])
        for i, (src, dst) in enumerate(
            [(routes_at, routes), (hinv_at, hinv), (down_at, down_w), (codes_at, codes), (scales_at, scales)]
        )
    ]
    small[0].start()
    own_tok.start()
    for one in small[1:]:
        one.start()
    own_gate.start()
    own_up.start()

    barrier = pltpu.get_barrier_semaphore()

    def greet(device):
        pl.semaphore_signal(barrier, inc=1, device_id=device, device_id_type=MESH)

    for dz in range(1, NZ):
        greet(far((z + dz) % NZ))

    @pl.when(c == 1)
    def _():
        greet(far(z))

    for yy in (y, yp, ym, yo):
        greet(peer(yy, xo))
    for yy in (yp, ym, yo):
        greet(peer(yy, xl))
    greet(sibling)

    small[0].wait()
    names = routes[...]
    experts = lax.broadcasted_iota(jnp.int32, (32, 128), 0)
    named = ((names[0:1, :] == experts) | (names[1:2, :] == experts)).astype(jnp.float32)
    earlier = (
        lax.broadcasted_iota(jnp.int32, (128, 128), 0) < lax.broadcasted_iota(jnp.int32, (128, 128), 1)
    ).astype(jnp.bfloat16)
    named_b = named.astype(jnp.bfloat16)
    rank = jnp.dot(named_b, earlier, preferred_element_type=jnp.float32)
    base = ((xh + c) % 2) * NZ
    slot = lax.broadcasted_iota(jnp.int32, (NZ * CAP, 32), 0)
    widen = (lax.broadcasted_iota(jnp.int32, (NZ * CAP, 32), 1) == base + slot // CAP).astype(jnp.bfloat16)
    rank_at = jnp.dot(widen, rank.astype(jnp.bfloat16), preferred_element_type=jnp.float32)
    named_at = jnp.dot(widen, named_b, preferred_element_type=jnp.float32)
    place = (lax.broadcasted_iota(jnp.int32, (NZ * CAP, 128), 0) % CAP).astype(jnp.float32)
    pick = jnp.where(rank_at == place, named_at, 0.0).astype(jnp.bfloat16)
    mine_of = (
        lax.broadcasted_iota(jnp.int32, (NZ, 32), 1) == base + lax.broadcasted_iota(jnp.int32, (NZ, 32), 0)
    ).astype(jnp.bfloat16)
    named_mine = jnp.dot(mine_of, named_b, preferred_element_type=jnp.float32)
    count[...] = jnp.dot(
        named_mine.astype(jnp.bfloat16), jnp.ones((128, 128), jnp.bfloat16), preferred_element_type=jnp.float32
    ).reshape(NZ, 1, 128)

    small[1].wait()
    small[2].wait()
    peers = NZ - 1 + CHIPS - 1 + 1

    @pl.when(c == 0)
    def _():
        pl.semaphore_wait(barrier, peers)

    @pl.when(c == 1)
    def _():
        pl.semaphore_wait(barrier, peers + 1)

    go(tokens, tok.at[half], AT_TOK, sibling)

    def cast(other):
        to = (e, jnp.int32(other))
        at = AT_CAST + 2 * FROM_ROOT.index(other)
        return copy(hinv, u_panel, AT_PANEL, to, at), copy(down_w, w_panel, AT_PANEL + 1, to, at + 1)

    @pl.when(f == 0)
    def _():
        for other in FROM_ROOT:
            for one in cast(other):
                one.start()
        u_panel[...] = hinv[...]
        w_panel[...] = down_w[...]

    own_tok.wait()
    arrived(tok.at[other_half], AT_TOK)
    packed[...] = (
        lax.dot_general(pick, tok[...], (((1,), (1,)), ((), ())), preferred_element_type=jnp.float32)
        .astype(jnp.bfloat16)
        .reshape(NZ, CAP, WIDE)
    )
    def landing(block):
        return rows.at[chip, pl.ds(block * CAP, CAP), :]

    def targets():
        for g in range(GROUPS):
            for j, dz in enumerate(Z_ORDER[g]):
                yield FIRST[g] + j, (z + dz) % NZ

    stay = pltpu.make_async_copy(packed.at[z], landing(0), local.at[3])
    cross_over = copy(packed.at[z], landing(0), AT_A2A, far(z))

    @pl.when(c == 0)
    def _():
        stay.start()

    @pl.when(c == 1)
    def _():
        cross_over.start()

    for block, z_to in targets():
        if block:
            go(packed.at[z_to], landing(block), AT_A2A + block, far(z_to))

    go(gate_w, weights.at[c, 0], AT_GATE, sibling)
    go(up_w, weights.at[c, 1], AT_UP, sibling)

    def dispatch_arrived(g):
        for block in range(FIRST[g], FIRST[g] + len(Z_ORDER[g])):
            if block == 0:

                @pl.when(c == 0)
                def _():
                    stay.wait()

                @pl.when(c == 1)
                def _():
                    arrived(landing(0), AT_A2A)
            else:
                arrived(landing(block), AT_A2A + block)

    def panel_to_sibling():
        @pl.when((c == 0) & (f != 0))
        def _():
            arrived(u_panel, AT_PANEL)
            arrived(w_panel, AT_PANEL + 1)

        @pl.when(c == 0)
        def _():
            copy(u_panel, u_panel, AT_PANEL, sibling).start()
            copy(w_panel, w_panel, AT_PANEL + 1, sibling).start()

    def counts_out():
        heard[0] = count[z]
        for block, z_to in targets():
            if block:
                go(count.at[z_to], heard.at[block], AT_COUNT + block, far(z_to))

        @pl.when(c == 1)
        def _():
            copy(count.at[z], heard.at[NZ], AT_COUNT, far(z)).start()

    def ring(piece, at, count_rows, width, cut):
        half_rows = count_rows // 2

        def part(yy, xx, first=0, count=count_rows, low=True, high=True):
            ref = piece(chip_of(yy, xx))
            start = 0 if low else cut
            stop = width if high else cut
            return ref.at[pl.ds(first, count), pl.ds(start, stop - start)]

        def send_own():
            mine = part(y, xl)
            go(mine, mine, at + 1, peer(yp, xl))
            go(mine, mine, at + 2, peer(ym, xl))
            go(mine, mine, at + 0, peer(y, xo))

        def second():
            arrived(part(y, xo), at + 0)
            low = part(y, xo, high=False)
            go(low, low, at + 5, peer(yp, xl))
            go(low, low, at + 6, peer(ym, xl))
            arrived(part(ym, xl), at + 1)
            on = part(ym, xl, 0, half_rows)
            go(on, on, at + 3, peer(yp, xl))
            cross = part(ym, xl, low=False)
            go(cross, cross, at + 9, peer(y, xo))
            arrived(part(yp, xl), at + 2)
            on = part(yp, xl, half_rows, half_rows)
            go(on, on, at + 4, peer(ym, xl))
            cross = part(yp, xl, low=False)
            go(cross, cross, at + 10, peer(y, xo))

        def third():
            arrived(part(ym, xo, high=False), at + 5)
            on = part(ym, xo, 0, half_rows, high=False)
            go(on, on, at + 7, peer(yp, xl))
            arrived(part(yp, xo, high=False), at + 6)
            on = part(yp, xo, half_rows, half_rows, high=False)
            go(on, on, at + 8, peer(ym, xl))
            arrived(part(yo, xl, 0, half_rows), at + 3)
            arrived(part(yo, xl, half_rows, half_rows), at + 4)
            cross = part(yo, xl, low=False)
            go(cross, cross, at + 11, peer(y, xo))

        def last():
            arrived(part(ym, xo, low=False), at + 9)
            arrived(part(yp, xo, low=False), at + 10)
            arrived(part(yo, xo, 0, half_rows, high=False), at + 7)
            arrived(part(yo, xo, half_rows, half_rows, high=False), at + 8)
            arrived(part(yo, xo, low=False), at + 11)

        return send_own, second, third, last

    def straight(piece, at):
        chips = [(dy, dx) for dy in (2, 1, 3, 0) for dx in (1, 0) if (dy, dx) != (0, 0)]

        def send_own():
            mine = piece(chip)
            for dy, dx in chips:
                go(mine, mine, at + dy * 2 + dx - 1, peer((y + dy) % NY, (xl + dx) % 2))

        def last():
            for dy, dx in chips:
                arrived(piece(chip_of((y + NY - dy) % NY, (xl + dx) % 2)), at + dy * 2 + dx - 1)

        def nothing():
            pass

        return send_own, nothing, nothing, last

    def hidden_units(g):
        if g == 0:
            own_gate.wait()
            own_up.wait()
            arrived(weights.at[1 - c, 0], AT_GATE)
            arrived(weights.at[1 - c, 1], AT_UP)
        span_g = pl.ds(FIRST[g] * CAP, ROWS[g])
        sums = jnp.zeros((ROWS[g], 2 * HID), jnp.float32)
        for s in range(CHIPS):
            span = pl.ds(s * WIDE, WIDE)
            factor = jnp.concatenate(
                [weights[0, 0, span, :], weights[1, 0, span, :], weights[0, 1, span, :], weights[1, 1, span, :]],
                axis=1,
            )
            sums += jnp.dot(rows[s, span_g, :], factor, preferred_element_type=jnp.float32)
        gate, up = sums[:, :HID], sums[:, HID:]
        hid[c, chip, span_g, :] = (gate / (1.0 + jnp.exp(-gate)) * up).astype(jnp.bfloat16)

    def group(g):
        span_g = pl.ds(FIRST[g] * CAP, ROWS[g])

        def row_piece(s):
            return rows.at[s, span_g, :]

        def hid_piece(s):
            return hid.at[c, s, span_g, :]

        if ROWS_RING[g]:
            send_own, second, third, last = ring(row_piece, AT_ROWS + RING * g, ROWS[g], WIDE, CUT)
        else:
            send_own, second, third, last = straight(row_piece, AT_ROWS + RING * g)
        if HID_RING[g]:
            h_own, h_second, h_third, h_last = ring(hid_piece, AT_HID + RING * g, ROWS[g], HID, HCUT)
        else:
            h_own, h_second, h_third, h_last = straight(hid_piece, AT_HID + RING * g)

        def start():
            dispatch_arrived(g)
            send_own()

        def compute():
            last()
            hidden_units(g)
            h_own()

        def pass_on():
            h_last()
            mine = hid.at[c, :, span_g, :]
            go(mine, mine, AT_SIB + g, sibling)

        def finish():
            arrived(hid.at[1 - c, :, span_g, :], AT_SIB + g)

        return start, second, third, compute, h_second, h_third, pass_on, finish

    def panel():
        @pl.when(c == 1)
        def _():
            arrived(u_panel, AT_PANEL)
            arrived(w_panel, AT_PANEL + 1)

        u = u_panel[...]
        r = lax.broadcasted_iota(jnp.int32, (128, 128), 0)
        q = lax.broadcasted_iota(jnp.int32, (128, 128), 1)
        on_diag = r == q
        inverse = jnp.where(on_diag, 1.0 / jnp.where(on_diag, u, 1.0), 0.0)
        size = 1
        while size < 128:
            block = jnp.where((r // (2 * size) == q // (2 * size)) & (r // size != q // size), u, 0.0)
            inverse = inverse - exact(exact(inverse, block), inverse)
            size *= 2
            yield
        small[3].wait()
        small[4].wait()
        steps = jnp.sum(jnp.where(on_diag, scales[...], 0.0), axis=1, keepdims=True)
        quant = steps * (codes[...] - 8).astype(jnp.float32)
        err = exact(w_panel[...].astype(jnp.float32) - quant, inverse)
        err_v[...] = err
        yield
        rest = down_w[...].astype(jnp.float32) - exact(err, hinv[...])
        down_v[...] = jnp.where(f == 0, quant, rest).astype(jnp.bfloat16)
        for one in results[:2]:
            one.start()

    columns = [pl.ds(s * HID, HID) for s in range(CHIPS)]
    results = [
        pltpu.make_async_copy(err_v, err_out, local.at[9]),
        pltpu.make_async_copy(down_v, down_out, local.at[10]),
    ] + [
        pltpu.make_async_copy(hess.at[:, columns[s]], hess_out.at[:, columns[s]], local.at[11 + s])
        for s in range(CHIPS)
    ]

    stages = [group(g) for g in range(GROUPS)]
    solve = panel()

    def run(*order):
        for who, what in order:
            if who == SOLVE:
                for _ in range(what):
                    next(solve, None)
            else:
                stages[who][what]()

    def products(start, count):
        def take(cc, at, width_at):
            return hid[cc, at, pl.ds(start, count), width_at]

        own = pl.ds(pl.multiple_of(c * COLS, COLS), COLS)
        mine = jnp.concatenate([take(0, chip, own), take(1, chip, own)], axis=0)
        for s in range(CHIPS):
            both = jnp.concatenate([take(0, s, slice(None)), take(1, s, slice(None))], axis=0)
            yield s, lax.dot_general(mine, both, (((0,), (0,)), ((), ())), preferred_element_type=jnp.float32)

    counts_out()
    run((0, 0))
    panel_to_sibling()
    run(
        (SOLVE, 4), (0, 1), (1, 0), (SOLVE, 2), (0, 2), (1, 1), (2, 0), (SOLVE, 2), (0, 3),
        (1, 2), (2, 1), (3, 0), (SOLVE, 1), (0, 4), (1, 3), (2, 2), (3, 1), (0, 5),
        (1, 4), (2, 3), (3, 2), (0, 6), (1, 5), (2, 4), (3, 3), (1, 6), (2, 5),
        (0, 7), (2, 6), (1, 7), (2, 7),
    )

    for block in range(1, NZ):
        arrived(heard.at[block], AT_COUNT + block)

    @pl.when(c == 1)
    def _():
        arrived(heard.at[NZ], AT_COUNT)

    own_count = jnp.sum(heard[1:NZ, 0], axis=0, keepdims=True) + jnp.where(c == 0, heard[0], heard[NZ])
    total[c] = jnp.broadcast_to(own_count, (8, 128))
    go(total.at[c], total.at[c], AT_TOTAL, sibling)
    for s, product in products(0, LATE):
        hess[:, columns[s]] = product
    run((3, 6))
    arrived(total.at[1 - c], AT_TOTAL)
    scale = 2.0 / (total[0, 0:1, :] + total[1, 0:1, :])
    scale = jnp.concatenate([scale, scale], axis=1)
    run((3, 7))
    for s, product in products(LATE, ROWS[-1]):
        hess[:, columns[s]] = scale * (hess[:, columns[s]] + product)
        results[2 + s].start()

    for src, at in sent:
        copy(src, src, at, sibling).wait_send()

    @pl.when(c == 1)
    def _():
        cross_over.wait_send()
        copy(count.at[z], heard.at[NZ], AT_COUNT, far(z)).wait_send()

    @pl.when(c == 0)
    def _():
        copy(u_panel, u_panel, AT_PANEL, sibling).wait_send()
        copy(w_panel, w_panel, AT_PANEL + 1, sibling).wait_send()

    @pl.when(f == 0)
    def _():
        for other in FROM_ROOT:
            for one in cast(other):
                one.wait_send()

    for one in results:
        one.wait()


def hand_on(hess, err, down, hess_out, err_out, down_out, hess_v, err_v, down_v, in_sems, out_sems):
    part = 32
    trips = [(err, err_v, err_out), (down, down_v, down_out)]
    for i in range(4):
        span = pl.ds(i * part, part)
        trips.append((hess.at[span], hess_v.at[span], hess_out.at[span]))
    loads = [pltpu.make_async_copy(src, here, in_sems.at[i]) for i, (src, here, _) in enumerate(trips)]
    stores = [pltpu.make_async_copy(here, dst, out_sems.at[i]) for i, (_, here, dst) in enumerate(trips)]
    for load in loads:
        load.start()
    for load, store in zip(loads, stores):
        load.wait()
        store.start()
    for store in stores:
        store.wait()


def body(tokens, routes, gate_w, up_w, down_w, codes, scales, hinv_panel):
    hbm = pl.BlockSpec(memory_space=pltpu.HBM)
    outs = (
        jax.ShapeDtypeStruct((COLS, 2048), jnp.float32),
        jax.ShapeDtypeStruct((128, 128), jnp.float32),
        jax.ShapeDtypeStruct((128, 128), jnp.bfloat16),
    )
    done = pl.pallas_call(
        kernel,
        out_shape=outs,
        in_specs=[hbm] * 8,
        out_specs=(hbm,) * 3,
        scratch_shapes=[
            pltpu.VMEM((COLS, 2048), jnp.float32),
            pltpu.VMEM((128, 128), jnp.float32),
            pltpu.VMEM((128, 128), jnp.bfloat16),
            pltpu.VMEM((2, 128), jnp.int32),
            pltpu.VMEM((128, 128), jnp.bfloat16),
            pltpu.VMEM((128, 128), jnp.int32),
            pltpu.VMEM((1, 128), jnp.float32),
            pltpu.VMEM((128, 128), jnp.float32),
            pltpu.VMEM((WIDE, 128), jnp.bfloat16),
            pltpu.VMEM((NZ, CAP, WIDE), jnp.bfloat16),
            pltpu.VMEM((CHIPS, NZ * CAP, WIDE), jnp.bfloat16),
            pltpu.VMEM((2, 2, CHIPS * WIDE, COLS), jnp.bfloat16),
            pltpu.VMEM((2, CHIPS, NZ * CAP, HID), jnp.bfloat16),
            pltpu.VMEM((128, 128), jnp.float32),
            pltpu.VMEM((128, 128), jnp.bfloat16),
            pltpu.VMEM((NZ, 1, 128), jnp.float32),
            pltpu.VMEM((NZ + 1, 1, 128), jnp.float32),
            pltpu.VMEM((2, 8, 128), jnp.float32),
            pltpu.SemaphoreType.DMA((N_SEND,)),
            pltpu.SemaphoreType.DMA((N_RECV,)),
            pltpu.SemaphoreType.DMA((N_LOCAL,)),
        ],
        compiler_params=pltpu.CompilerParams(
            collective_id=0, has_side_effects=True, vmem_limit_bytes=62 * 1024 * 1024
        ),
        cost_estimate=pl.CostEstimate(flops=2_200_000_000, bytes_accessed=16_000_000, transcendentals=65536),
        name="calibrate",
    )(routes.T, tokens.T, gate_w[0], up_w[0], down_w[0], codes[0], scales, hinv_panel[0])
    hess, err, down = pl.pallas_call(
        hand_on,
        out_shape=outs,
        in_specs=[hbm] * 3,
        out_specs=(hbm,) * 3,
        scratch_shapes=[
            pltpu.VMEM((COLS, 2048), jnp.float32),
            pltpu.VMEM((128, 128), jnp.float32),
            pltpu.VMEM((128, 128), jnp.bfloat16),
            pltpu.SemaphoreType.DMA((6,)),
            pltpu.SemaphoreType.DMA((6,)),
        ],
        name="hand_on",
    )(*done)
    return hess[None], err[None], down[None]


def solution(mesh):
    return jax.shard_map(
        body,
        mesh=mesh,
        in_specs=(
            P("expert", "ffn"),
            P("expert", None),
            P("expert", None, "ffn"),
            P("expert", None, "ffn"),
            P("expert", None, "ffn"),
            P("expert", None, None),
            P("expert", None),
            P("expert", None, "ffn"),
        ),
        out_specs=(P("expert", "ffn", None), P("expert", None, None), P("expert", None, "ffn")),
        check_vma=False,
    )
```

time: 88.4 us -> 75.6 us (0.86)
  Pallas kernels: 84 us -> 74.8 us
  local copies, waits for them, and re-layouts: 3.58 us -> 0 us
    pallas_call x1 -> x2, Pallas kernels: 84 us -> 74.8 us  [the longest x1 72.7 us: body(): pl.pallas_call(kernel, out_shape=outs, in_specs=[hbm] * 8, out_specs=(hbm...]
    unnamed x7 -> x0, local copies, waits for them, and re-layouts: 3.58 us -> none
where the time goes in v2:
time: 75.6 us; the launch traced here: 75.5 us
  Pallas kernels  74.8 us (99%)
    pallas_call x1, Pallas kernels, body(): pl.pallas_call(kernel, out_shape=outs, in_specs=[hbm] * 8, out_specs=(hbm...  72.7 us
    pallas_call x1, Pallas kernels, body(): pl.pallas_call(hand_on, out_shape=outs, in_specs=[hbm] * 3, out_specs=(hb...  2.07 us

profile of v2, /device:TPU:1, one launch (start us, length us, event | category | flops | bytes accessed | tf_op | source)
XLA Modules:
  0.0 75.5 jit_solution(15223357605711174645)
XLA Ops:
  0.6 72.7 %calibrate.1 = (f32[128,2048]{1,0:T(8,128)}, f32[128,128]{1,0:T(8,128)}, bf16[128,128]{1,0:T(8,128)(2,1)}) custom-call(s32[2,128]{1,0:T(2,128)} %bitcast.19, bf16[448,128]{1,0:T(8,128)(2,1)} %bitcast.13, bf16[7168,128]{1,0:T(8,128)(2,1)} %bitcast.10, bf16[7168,128]{1,0:T(8,128)(2,1)} %bitcast.11, bf16[128,128]{1,0:T(8,128)(2,1)} %bitcast.17, ...), custom_call_target="tpu_custom_call" | custom-call | flops 2200000000 | bytes 16000000 | tf_op jit(solution)/shard_map/calibrate/pallas_call | solution.py:510
  73.4 2.1 %hand_on.1 = (f32[128,2048]{1,0:T(8,128)}, f32[128,128]{1,0:T(8,128)}, bf16[128,128]{1,0:T(8,128)(2,1)}) custom-call(f32[128,2048]{1,0:T(8,128)} %get-tuple-element.9.hess, f32[128,128]{1,0:T(8,128)} %get-tuple-element.10.err, bf16[128,128]{1,0:T(8,128)(2,1)} %get-tuple-element.11.down), custom_call_target="tpu_custom_call" | custom-call | tf_op jit(solution)/shard_map/hand_on/pallas_call | solution.py:544

commit v3 on v2

--- a/solution.py
+++ b/solution.py
@@ -315,23 +315,29 @@
 
         return send_own, nothing, nothing, last
 
-    def hidden_units(g):
+    def weighed(g, chips):
+        sums = jnp.zeros((ROWS[g], 2 * HID), jnp.float32)
+        for s in chips:
+            span = pl.ds(pl.multiple_of(s * WIDE, WIDE), WIDE)
+            factor = jnp.concatenate(
+                [weights[0, 0, span, :], weights[1, 0, span, :], weights[0, 1, span, :], weights[1, 1, span, :]],
+                axis=1,
+            )
+            piece = rows[s, pl.ds(FIRST[g] * CAP, ROWS[g]), :]
+            sums += jnp.dot(piece, factor, preferred_element_type=jnp.float32)
+        return sums
+
+    def hidden_units(g, last):
         if g == 0:
             own_gate.wait()
             own_up.wait()
             arrived(weights.at[1 - c, 0], AT_GATE)
             arrived(weights.at[1 - c, 1], AT_UP)
-        span_g = pl.ds(FIRST[g] * CAP, ROWS[g])
-        sums = jnp.zeros((ROWS[g], 2 * HID), jnp.float32)
-        for s in range(CHIPS):
-            span = pl.ds(s * WIDE, WIDE)
-            factor = jnp.concatenate(
-                [weights[0, 0, span, :], weights[1, 0, span, :], weights[0, 1, span, :], weights[1, 1, span, :]],
-                axis=1,
-            )
-            sums += jnp.dot(rows[s, span_g, :], factor, preferred_element_type=jnp.float32)
+        early = weighed(g, [chip, chip_of(y, xo), chip_of(ym, xl), chip_of(yp, xl), chip_of(yo, xl)])
+        last()
+        sums = early + weighed(g, [chip_of(ym, xo), chip_of(yp, xo), chip_of(yo, xo)])
         gate, up = sums[:, :HID], sums[:, HID:]
-        hid[c, chip, span_g, :] = (gate / (1.0 + jnp.exp(-gate)) * up).astype(jnp.bfloat16)
+        hid[c, chip, pl.ds(FIRST[g] * CAP, ROWS[g]), :] = (gate / (1.0 + jnp.exp(-gate)) * up).astype(jnp.bfloat16)
 
     def group(g):
         span_g = pl.ds(FIRST[g] * CAP, ROWS[g])
@@ -356,8 +362,7 @@
             send_own()
 
         def compute():
-            last()
-            hidden_units(g)
+            hidden_units(g, last)
             h_own()
 
         def pass_on():

time: 75.6 us -> 74.7 us (0.988)
  Pallas kernels: 74.8 us -> 73.9 us
    pallas_call x1, Pallas kernels: 72.7 us -> 71.9 us  [body(): pl.pallas_call(kernel, out_shape=outs, in_specs=[hbm] * 8, out_specs=(hbm...]
where the time goes in v3:
time: 74.7 us; the launch traced here: 74.6 us
  Pallas kernels  73.9 us (99%)
    pallas_call x1, Pallas kernels, body(): pl.pallas_call(kernel, out_shape=outs, in_specs=[hbm] * 8, out_specs=(hbm...  71.9 us
    pallas_call x1, Pallas kernels, body(): pl.pallas_call(hand_on, out_shape=outs, in_specs=[hbm] * 3, out_specs=(hb...  2.07 us

profile of v3, /device:TPU:1, one launch (start us, length us, event | category | flops | bytes accessed | tf_op | source)
XLA Modules:
  0.0 74.6 jit_solution(3558463000558914835)
XLA Ops:
  0.6 71.9 %calibrate.1 = (f32[128,2048]{1,0:T(8,128)}, f32[128,128]{1,0:T(8,128)}, bf16[128,128]{1,0:T(8,128)(2,1)}) custom-call(s32[2,128]{1,0:T(2,128)} %bitcast.19, bf16[448,128]{1,0:T(8,128)(2,1)} %bitcast.13, bf16[7168,128]{1,0:T(8,128)(2,1)} %bitcast.10, bf16[7168,128]{1,0:T(8,128)(2,1)} %bitcast.11, bf16[128,128]{1,0:T(8,128)(2,1)} %bitcast.17, ...), custom_call_target="tpu_custom_call" | custom-call | flops 2200000000 | bytes 16000000 | tf_op jit(solution)/shard_map/calibrate/pallas_call | solution.py:515
  72.5 2.1 %hand_on.1 = (f32[128,2048]{1,0:T(8,128)}, f32[128,128]{1,0:T(8,128)}, bf16[128,128]{1,0:T(8,128)(2,1)}) custom-call(f32[128,2048]{1,0:T(8,128)} %get-tuple-element.9.hess, f32[128,128]{1,0:T(8,128)} %get-tuple-element.10.err, bf16[128,128]{1,0:T(8,128)(2,1)} %get-tuple-element.11.down), custom_call_target="tpu_custom_call" | custom-call | tf_op jit(solution)/shard_map/hand_on/pallas_call | solution.py:549
